TPU v7x, 32 devices: a whole 2x2x4 slice. The times are simulated.
32 devices in a mesh: grp: 2 (over y), dp: 4 (over z), tensor: 4 (over x, core).
Axes of the slice: x: 2, y: 2, z: 4, core: 2. Of those that a mesh axis runs over, the one named last changes fastest.
Arguments:
- queries: bfloat16 [256, 8192], P(('grp', 'dp'), 'tensor'), parts along dimension 0, may hold values from -128 to 128
- key_value_cache: bfloat16 [256, 8, 2, 1024], P(('grp', 'dp'), None, None, 'tensor'), parts along dimension 0, may hold values from -7 to 7
- key_value_lengths: int32 [256], P(('grp', 'dp')), parts along dimension 0, may hold values from 1 to 8, as said below
- adapter_index: int32 [256], P(('grp', 'dp')), parts along dimension 0, may hold values from 0 to 3, as said below
- adapter_down_weight: bfloat16 [4, 64, 8192], P('dp', None, 'tensor'), may hold values from -0.0625 to 0.0625
- adapter_up_weight: bfloat16 [4, 64, 8192], P(None, None, 'dp'), may hold values from -0.75 to 0.75
- output_weight: bfloat16 [8192, 8192], P('tensor', 'dp'), may hold values from -0.0625 to 0.0625
Outputs:
- mixed: bfloat16 [256, 8192], P(('grp', 'tensor'), 'dp'), parts along dimension 0
- moved_cache: bfloat16 [512, 8, 2, 1024], P(('grp', 'dp'), None, None, 'tensor'), parts along dimension 0
There are 2 independent parts, one for each index of `grp`. A program takes and returns all parts, laid end to end along the dimension named above; an argument that names none is the same for every part. Nothing has to cross between parts.
Inputs may be any that keep to these rules, and one draw needn't show every extreme that they name: `adapter_index`: among the 32 requests of one home rank at most 16 name the same adapter. `key_value_lengths`: the largest is 8.
All inputs are finite; a program needn't handle non-finite values.
Results may differ from a plain program's by a relative error of at most 0.0065.
Values may be sent and summed in bfloat16 or wider, within the bound.
A program may use at most 64 MiB of HBM per device.

v0:
```python
import math

import jax
import jax.numpy as jnp
from jax import lax
from jax.sharding import PartitionSpec as P

HD = 128


def earlier_same(targets):
    count = targets.shape[0]
    order = jnp.arange(count, dtype=jnp.int32)
    same = targets[:, None] == targets[None, :]
    before = order[None, :] < order[:, None]
    return jnp.sum(jnp.where(same & before, 1, 0), axis=1).astype(jnp.int32)


def attend(queries, cache, lengths):
    count = queries.shape[0]
    width = cache.shape[-1]
    kv_heads = width // HD
    group = queries.shape[1] // width
    query = queries.reshape(count, kv_heads, group, HD)
    keys = cache[:, :, 0, :].reshape(count, -1, kv_heads, HD)
    values = cache[:, :, 1, :].reshape(count, -1, kv_heads, HD)
    scores = jnp.einsum("rhgd,rlhd->rhgl", query, keys, preferred_element_type=jnp.float32) * (
        1.0 / math.sqrt(HD)
    )
    position = jnp.arange(keys.shape[1], dtype=jnp.int32)
    live = position[None, None, None, :] < lengths[:, None, None, None]
    scores = jnp.where(live, scores, -1e30)
    highest = jnp.max(scores, axis=-1, keepdims=True)
    powers = jnp.exp(scores - highest)
    weights = (powers / jnp.sum(powers, axis=-1, keepdims=True)).astype(jnp.bfloat16)
    output = jnp.einsum("rhgl,rlhd->rhgd", weights, values, preferred_element_type=jnp.float32)
    return output.reshape(count, -1).astype(jnp.bfloat16)


def down_projection(attended_rows, adapter_down_weight):
    product = lax.dot_general(
        attended_rows,
        adapter_down_weight[0],
        (((1,), (1,)), ((), ())),
        preferred_element_type=jnp.float32,
    )
    return product.astype(jnp.bfloat16)


def shards(
    queries,
    key_value_cache,
    key_value_lengths,
    adapter_index,
    adapter_down_weight,
    adapter_up_weight,
    output_weight,
):
    peers = lax.axis_size("dp")
    count = queries.shape[0]
    capacity = max(2, 2 * count // peers)
    slots = peers * capacity
    places = adapter_index * capacity + earlier_same(adapter_index)

    def spread(values):
        return jnp.zeros((slots,) + values.shape[1:], values.dtype).at[places].set(values)

    attended_rows = attend(queries, key_value_cache, key_value_lengths)
    moved_attended, moved_cache = (
        lax.all_to_all(spread(attended_rows), "dp", split_axis=0, concat_axis=0, tiled=True),
        lax.all_to_all(spread(key_value_cache), "dp", split_axis=0, concat_axis=0, tiled=True),
    )
    low_rank_output = down_projection(moved_attended, adapter_down_weight)
    lowered = lax.all_to_all(low_rank_output, "dp", split_axis=0, concat_axis=0, tiled=True)[places]
    adapter_table = adapter_up_weight.shape[0]
    device_rank = adapter_up_weight.shape[1]
    flattened_up = adapter_up_weight.reshape(
        adapter_table * device_rank, adapter_up_weight.shape[2]
    )
    part_attended = lax.all_gather(attended_rows, "dp", axis=0, tiled=True)
    part_lowered = lax.all_gather(lowered, "dp", axis=0, tiled=True)
    part_ids = lax.all_gather(adapter_index, "dp", axis=0, tiled=True)
    height = part_attended.shape[0]
    chosen = part_ids[:, None] == jnp.arange(adapter_table, dtype=jnp.int32)[None, :]
    expanded = jnp.where(chosen[:, :, None], part_lowered[:, None, :], jnp.zeros((), jnp.bfloat16))
    expanded = expanded.reshape(height, adapter_table * device_rank)
    request_block = jnp.dot(part_attended, output_weight, preferred_element_type=jnp.float32)
    request_block = request_block + jnp.dot(
        expanded, flattened_up, preferred_element_type=jnp.float32
    )
    mixed = lax.psum_scatter(request_block, "tensor", scatter_dimension=0, tiled=True).astype(
        jnp.bfloat16
    )
    return (mixed, moved_cache)


def solution(mesh):
    in_specs = (
        P(("grp", "dp"), "tensor"),
        P(("grp", "dp"), None, None, "tensor"),
        P(("grp", "dp")),
        P(("grp", "dp")),
        P("dp", None, "tensor"),
        P(None, None, "dp"),
        P("tensor", "dp"),
    )
    out_specs = (P(("grp", "tensor"), "dp"), P(("grp", "dp"), None, None, "tensor"))
    return jax.shard_map(shards, mesh=mesh, in_specs=in_specs, out_specs=out_specs, check_vma=False)
```

profile of v0, /device:TPU:0, one launch (start us, length us, event | category | flops | bytes accessed | tf_op | source)
XLA Modules:
  0.0 111.5 jit_solution(10252538007645904782)
XLA Ops:
  7.2 0.0 copy-start
  7.2 1.6 %fusion.15 = (bf16[32,8,1,256]{3,2,1,0:T(2,128)(2,1)S(1)}, bf16[32,8,1,256]{3,2,1,0:T(2,128)(2,1)S(1)}) fusion(bf16[32,8,2,256]{3,2,1,0:T(2,128)(2,1)} %param.8), kind=kLoop, calls=%fused_computation.32 | loop fusion | bytes 524288 | tf_op jit(solution)/shard_map/slice | solution.py:25
  8.8 0.9 copy.28
  9.7 0.7 iota_compare_fusion.1
  10.4 0.2 fusion.3
  10.6 0.2 fusion.16
  10.8 0.9 select_reduce_fusion
  11.7 0.7 compare_select_fusion
  12.4 0.3 convolution_convert_fusion
  12.7 1.5 %scatter_custom_fusion = bf16[64,2048]{1,0:T(8,128)(2,1)} fusion(s32[32]{0:T(128)S(1)} %compare_select_fusion, bf16[]{:T(256)} %constant.1.clone.1, bf16[4,8,16,128]{3,2,1,0:T(8,128)(2,1)S(1)} %bitcast.36), kind=kCustom, calls=%fused_computation.17 | custom fusion | bytes 393218 | tf_op jit(solution)/shard_map/scatter | solution.py:66
  14.2 0.0 copy-start.2
  14.2 6.5 %all-to-all-start = ((bf16[4,16,2048]{2,1,0:T(8,128)(2,1)}), bf16[4,16,2048]{2,1,0:T(8,128)(2,1)S(1)}, u32[]{:S(2)}, u32[]{:S(2)}) async-start(bf16[4,16,2048]{2,1,0:T(8,128)(2,1)} %bitcast.3), calls=%async_computation | async-start | bytes 524288 | tf_op jit(solution)/shard_map/all_to_all | solution.py:70
  20.7 19.7 %all_gather.9 = bf16[128,2048]{1,0:T(8,128)(2,1)S(1)} all-gather(bf16[32,2048]{1,0:T(8,128)(2,1)S(1)} %bitcast.35), channel_id=1, replica_groups=mesh['grp'=2,'dp'=4,'tensor'=4] {'dp'}, dimensions={0}, use_global_device_ids=true | all-gather | bytes 655360 | tf_op jit(solution)/shard_map/all_gather | solution.py:80
  40.5 1.2 %dynamic-slice = u32[1]{0:T(128)} dynamic-slice(u32[32]{0:T(128)} %constant.24, u32[]{:T(128)S(6)} %add.16), dynamic_slice_sizes={1} | dynamic-slice | bytes 12
  42.4 0.9 dynamic-update-slice
  43.2 6.6 %all-reduce = s32[128]{0:T(128)S(1)} all-reduce(s32[128]{0:T(128)S(1)} %dynamic-update-slice), channel_id=1, replica_groups=mesh['grp'=2,'dp'=4,'tensor'=4] {'dp'}, use_global_device_ids=true, to_apply=%add | all-reduce | flops 128 | bytes 1024
  49.8 0.0 copy-start.1
  49.8 4.7 %fusion.17 = f32[128,2048]{1,0:T(8,128)S(1)} fusion(bf16[128,2048]{1,0:T(8,128)(2,1)S(1)} %all_gather.9, bf16[2048,2048]{1,0:T(8,128)(2,1)} %param.13), kind=kOutput, calls=%fused_computation.34 | convolution fusion | flops 1073741824 | bytes 9961472 | tf_op jit(solution)/shard_map/dot_general | solution.py:87
  54.5 0.0 all-to-all-done
  54.5 0.0 copy-done.2
  54.5 0.2 convolution_convert_fusion.1
  54.7 0.7 reshape.99
  55.4 3.5 %all-to-all-start.1 = ((bf16[4,2,512]{2,1,0:T(2,128)(2,1)}), bf16[4,2,512]{2,1,0:T(2,128)(2,1)S(1)}, u32[]{:S(2)}, u32[]{:S(2)}) async-start(bf16[4,2,512]{2,1,0:T(2,128)(2,1)} %reshape.99), calls=%async_computation.1 | async-start | bytes 16384 | tf_op jit(solution)/shard_map/all_to_all | solution.py:74
  58.9 0.0 reduce-scatter.2.cloned.1.call-start
  58.9 5.6 %all-to-all-done.1 = bf16[4,2,512]{2,1,0:T(2,128)(2,1)S(1)} async-done(((bf16[4,2,512]{2,1,0:T(2,128)(2,1)}), bf16[4,2,512]{2,1,0:T(2,128)(2,1)S(1)}, u32[]{:S(2)}, u32[]{:S(2)}) %all-to-all-start.1) | async-done | bytes 8224 | tf_op jit(solution)/shard_map/all_to_all | solution.py:74
  64.5 0.1 reshape.100
  64.6 0.6 gather_fusion
  65.2 13.1 %all-gather = bf16[128,64]{1,0:T(8,128)(2,1)S(1)} all-gather(bf16[32,64]{1,0:T(8,128)(2,1)S(1)} %gather_fusion), channel_id=2, replica_groups=mesh['grp'=2,'dp'=4,'tensor'=4] {'dp'}, dimensions={0}, use_global_device_ids=true | all-gather | bytes 20480 | tf_op jit(solution)/shard_map/all_gather | solution.py:81
  78.3 0.1 copy.22
  78.4 0.0 copy-done
  78.4 1.3 %fusion.1 = f32[128,2048]{1,0:T(8,128)} fusion(f32[128,2048]{1,0:T(8,128)S(1)} %fusion.17, bf16[4,64,2048]{2,1,0:T(8,128)(2,1)S(1)} %copy-done, pred[128,4]{0,1:T(4,128)(4,1)S(1)} %iota_compare_fusion.2, bf16[128,64]{0,1:T(8,128)(2,1)S(1)} %copy.22), kind=kOutput, calls=%fused_computation.5 | convolution fusion | flops 134512640 | bytes 3162624 | tf_op jit(solution)/shard_map/dot_general | solution.py:88
  79.7 0.0 reduce-scatter.2.cloned.1.call-update
  79.7 0.0 copy-done.1
  79.8 1.5 %scatter_fusion = bf16[64,8,2,256]{3,1,2,0:T(8,128)(2,1)S(1)} fusion(bf16[64,8,2,256]{3,1,2,0:T(8,128)(2,1)S(1)} %broadcast_in_dim.72, s32[32]{0:T(128)S(1)} %compare_select_fusion, bf16[32,8,2,256]{3,1,2,0:T(8,128)(2,1)S(1)} %copy.23), kind=kCustom, calls=%fused_computation.2 | custom fusion | bytes 786560 | tf_op jit(solution)/shard_map/scatter | solution.py:66
  81.3 12.7 %all_to_all.29 = bf16[64,8,2,256]{3,1,2,0:T(8,128)(2,1)S(1)} all-to-all(bf16[64,8,2,256]{3,1,2,0:T(8,128)(2,1)S(1)} %scatter_fusion), channel_id=1, replica_groups=mesh['grp'=2,'dp'=4,'tensor'=4] {'dp'}, dimensions={0} | all-to-all | bytes 1048576 | tf_op jit(solution)/shard_map/all_to_all | solution.py:71
  94.0 1.2 %copy.24 = bf16[64,8,2,256]{3,2,1,0:T(2,128)(2,1)} copy(bf16[64,8,2,256]{3,1,2,0:T(8,128)(2,1)S(1)} %all_to_all.29) | data formatting | bytes 1048576
  95.2 7.8 %reduce-scatter.2.cloned.1.call-done = f32[32,2048]{1,0:T(8,128)} async-done(((f32[128,2048]{1,0:T(8,128)}), f32[32,2048]{1,0:T(8,128)}) %reduce-scatter.2.cloned.1.call-update) | async-done | bytes 262160 | tf_op jit(solution)/shard_map/reduce_scatter | solution.py:91
  103.1 1.6 %convert_element_type.19 = bf16[32,2048]{1,0:T(8,128)(2,1)} convert(f32[32,2048]{1,0:T(8,128)} %reduce-scatter.2.cloned.1.call-done) | non-fusion elementwise | flops 65536 | bytes 393216 | tf_op jit(solution)/shard_map/convert_element_type | solution.py:91
  (6 shorter events, 0.1 us)
Async XLA Ops:
  7.2 71.2 %copy-start = (bf16[4,64,2048]{2,1,0:T(8,128)(2,1)S(1)}, bf16[4,64,2048]{2,1,0:T(8,128)(2,1)}, u32[]{:S(2)}) copy-start(bf16[4,64,2048]{2,1,0:T(8,128)(2,1)} %param.12) | copy-start | bytes 3145732
  14.2 40.3 %copy-start.2 = (bf16[1,64,2048]{2,1,0:T(8,128)(2,1)S(1)}, bf16[1,64,2048]{2,1,0:T(8,128)(2,1)}, u32[]{:S(2)}) copy-start(bf16[1,64,2048]{2,1,0:T(8,128)(2,1)} %param.11) | copy-start | bytes 786436
  14.2 40.3 %all-to-all-start = ((bf16[4,16,2048]{2,1,0:T(8,128)(2,1)}), bf16[4,16,2048]{2,1,0:T(8,128)(2,1)S(1)}, u32[]{:S(2)}, u32[]{:S(2)}) async-start(bf16[4,16,2048]{2,1,0:T(8,128)(2,1)} %bitcast.3), calls=%async_computation | async-start | bytes 524288 | tf_op jit(solution)/shard_map/all_to_all | solution.py:70
  49.8 29.9 %copy-start.1 = (bf16[32,8,2,256]{3,2,1,0:T(2,128)(2,1)S(1)}, bf16[32,8,2,256]{3,2,1,0:T(2,128)(2,1)}, u32[]{:S(2)}) copy-start(bf16[32,8,2,256]{3,2,1,0:T(2,128)(2,1)} %param.8) | copy-start | bytes 786436
  55.4 9.0 %all-to-all-start.1 = ((bf16[4,2,512]{2,1,0:T(2,128)(2,1)}), bf16[4,2,512]{2,1,0:T(2,128)(2,1)S(1)}, u32[]{:S(2)}, u32[]{:S(2)}) async-start(bf16[4,2,512]{2,1,0:T(2,128)(2,1)} %reshape.99), calls=%async_computation.1 | async-start | bytes 16384 | tf_op jit(solution)/shard_map/all_to_all | solution.py:74
  58.9 44.2 %reduce-scatter.2.cloned.1.call-start = ((), (), s32[]{:S(2)}) async-start(), calls=%async_computation.4 | async-start | bytes 1310720 | tf_op jit(solution)/shard_map/reduce_scatter | solution.py:91
Sparse Core Ops, SparseCore 0:
  79.9 23.1 reduce-scatter.1
where the time goes:
time: 112 us
  blocking collectives  52.1 us (47%)
  between operations  14.8 us (13%)
  waiting for transfers between devices  13.4 us (12%)
  local copies, waits for them, and re-layouts  10.4 us (9%)
  starting transfers between devices  9.91 us (9%)
  matrix products  6.74 us (6%)
  other arithmetic  4.13 us (4%)
    all_gather x1, blocking collectives, shards(): part_attended = lax.all_gather(attended_rows, 'dp', axis=0, tiled=True)  19.7 us
    all_gather x1, blocking collectives, shards(): part_lowered = lax.all_gather(lowered, 'dp', axis=0, tiled=True)  13.1 us
    all_to_all x1, blocking collectives, shards(): lax.all_to_all(spread(key_value_cache), 'dp', split_axis=0, concat_axis=0...  12.7 us
    reduce_scatter x1, waiting for transfers between devices, shards(): lax.psum_scatter(request_block, 'tensor', scatter_dimension=0, tiled=True)  7.82 us
    unnamed x1, blocking collectives  6.59 us
    all_to_all x1, starting transfers between devices, shards(): lax.all_to_all(spread(attended_rows), 'dp', split_axis=0, concat_axis=0,...  6.45 us
    all_to_all x1, waiting for transfers between devices, shards(): lax.all_to_all(low_rank_output, 'dp', split_axis=0, concat_axis=0, tiled=...  5.58 us
    unnamed x15, local copies, waits for them, and re-layouts  5.09 us
  transfers between devices with their start and end apart: 3, of which 2 were waited for; matrix products, arithmetic and copies ran while one was open for 9% of the time, Pallas kernels for 0%

commit v1 on v0

--- a/solution.py
+++ b/solution.py
@@ -1,11 +1,307 @@
+import functools
 import math
 
 import jax
 import jax.numpy as jnp
 from jax import lax
+from jax.experimental import pallas as pl
+from jax.experimental.pallas import tpu as pltpu
 from jax.sharding import PartitionSpec as P
 
 HD = 128
+LANES = 128
+MESH = pl.DeviceIdType.MESH
+F32 = jnp.float32
+BF16 = jnp.bfloat16
+
+
+def nt_dot(a, b):
+    return lax.dot_general(a, b, (((1,), (1,)), ((), ())), preferred_element_type=F32)
+
+
+def dot(a, b):
+    return jnp.dot(a, b, preferred_element_type=F32)
+
+
+def iota(shape, axis):
+    return lax.broadcasted_iota(jnp.int32, shape, axis)
+
+
+def flag(cond):
+    return jnp.where(cond, 1.0, 0.0).astype(BF16)
+
+
+def fused_kernel(
+    peers,
+    blocks,
+    width,
+    q_ref,
+    cache_ref,
+    len_ref,
+    id_ref,
+    down_hbm,
+    up_hbm,
+    w_hbm,
+    mixed_ref,
+    moved_ref,
+    w_buf,
+    up_buf,
+    down_buf,
+    att_buf,
+    spread_buf,
+    low_buf,
+    base_buf,
+    part_buf,
+    part_recv,
+    load_sem,
+    att_send,
+    att_recv,
+    cache_send,
+    cache_recv,
+    low_send,
+    low_recv,
+    part_send_sem,
+    part_recv_sem,
+):
+    dp = lax.axis_index("dp")
+    tp = lax.axis_index("tensor")
+    count, feats = q_ref.shape
+    capacity = spread_buf.shape[1]
+    out_width = w_buf.shape[1]
+    chunks = part_recv.shape[0]
+    chunk = out_width // chunks
+    kv_heads = width // HD
+    group = feats // width
+    positions = cache_ref.shape[1] // (2 * width)
+
+    loads = [
+        pltpu.make_async_copy(down_hbm, down_buf, load_sem.at[0]),
+        pltpu.make_async_copy(w_hbm, w_buf, load_sem.at[1]),
+        pltpu.make_async_copy(up_hbm, up_buf, load_sem.at[2]),
+    ]
+    for load in loads:
+        load.start()
+
+    barrier = pltpu.get_barrier_semaphore()
+    for d in range(1, peers):
+        pl.semaphore_signal(
+            barrier, inc=1, device_id={"dp": lax.rem(dp + d, peers)}, device_id_type=MESH
+        )
+    for d in range(1, blocks):
+        pl.semaphore_signal(
+            barrier, inc=1, device_id={"tensor": lax.rem(tp + d, blocks)}, device_id_type=MESH
+        )
+
+    rows, cols = group * count, positions * count
+    row_request = iota((rows, cols), 0) & (count - 1)
+    col_index = iota((rows, cols), 1)
+    col_request = col_index & (count - 1)
+    tile_requests = flag(
+        iota((count, cols), 0) == (iota((count, cols), 1) & (count - 1))
+    )
+    lengths = jnp.broadcast_to(len_ref[...], (16, count)).astype(F32).astype(BF16)
+    limit = dot(lengths, tile_requests)[0:1, :] * float(count)
+    live = (row_request == col_request) & (col_index.astype(F32) < limit)
+    for g in range(kv_heads):
+        query = jnp.concatenate(
+            [q_ref[:, (g * group + h) * HD : (g * group + h + 1) * HD] for h in range(group)], 0
+        )
+        keys = jnp.concatenate(
+            [
+                cache_ref[:, 2 * j * width + g * HD : 2 * j * width + (g + 1) * HD]
+                for j in range(positions)
+            ],
+            0,
+        )
+        values = jnp.concatenate(
+            [
+                cache_ref[:, (2 * j + 1) * width + g * HD : (2 * j + 1) * width + (g + 1) * HD]
+                for j in range(positions)
+            ],
+            0,
+        )
+        scores = jnp.where(live, nt_dot(query, keys) * (1.0 / math.sqrt(HD)), -1e30)
+        powers = jnp.exp(scores - jnp.max(scores, axis=1, keepdims=True))
+        weights = (powers / jnp.sum(powers, axis=1, keepdims=True)).astype(BF16)
+        output = dot(weights, values).astype(BF16)
+        for h in range(group):
+            att_buf[dp, :, (g * group + h) * HD : (g * group + h + 1) * HD] = output[
+                h * count : (h + 1) * count
+            ]
+
+    ids = jnp.broadcast_to(id_ref[...], (LANES, count))
+    chosen = iota((LANES, count), 0) == ids
+    chosen_flag = flag(chosen)
+    eye = flag(iota((count, count), 0) == iota((count, count), 1))
+    att_buf[dp, :, feats : feats + LANES] = nt_dot(eye, chosen_flag).astype(BF16)
+
+    pl.semaphore_wait(barrier, peers - 1 + blocks - 1)
+    att_copies = []
+    for d in range(1, peers):
+        copy = pltpu.make_async_remote_copy(
+            src_ref=att_buf.at[dp],
+            dst_ref=att_buf.at[dp],
+            send_sem=att_send.at[d - 1],
+            recv_sem=att_recv.at[d - 1],
+            device_id={"dp": lax.rem(dp + d, peers)},
+            device_id_type=MESH,
+        )
+        copy.start()
+        att_copies.append(copy)
+
+    earlier = flag(iota((count, count), 0) < iota((count, count), 1))
+    before = dot(chosen_flag, earlier)
+    rank = jnp.sum(jnp.where(chosen, before, 0.0), axis=0, keepdims=True)
+    place = id_ref[...].astype(F32) * float(capacity) + rank
+    slots = peers * capacity
+    move = flag(iota((slots, count), 0).astype(F32) == place)
+    step = 512
+    for c in range(cache_ref.shape[1] // step):
+        piece = dot(move, cache_ref[:, c * step : (c + 1) * step]).astype(BF16)
+        spread_buf[:, :, c * step : (c + 1) * step] = piece.reshape(peers, capacity, step)
+    cache_copies = []
+    for d in range(1, peers):
+        target = lax.rem(dp + d, peers)
+        copy = pltpu.make_async_remote_copy(
+            src_ref=spread_buf.at[target],
+            dst_ref=moved_ref.at[dp],
+            send_sem=cache_send.at[d - 1],
+            recv_sem=cache_recv.at[d - 1],
+            device_id={"dp": target},
+            device_id_type=MESH,
+        )
+        copy.start()
+        cache_copies.append(copy)
+    own = pltpu.make_async_copy(spread_buf.at[dp], moved_ref.at[dp], load_sem.at[3])
+    own.start()
+
+    for copy in att_copies:
+        copy.wait_recv()
+    height = peers * count
+    att = att_buf[:, :, :feats].reshape(height, feats)
+    member = att_buf[:, :, feats : feats + LANES].reshape(height, LANES)
+    loads[0].wait()
+    low_rank = down_buf.shape[1]
+    held = flag(iota((LANES, low_rank), 0) == dp)
+    low = nt_dot(att, down_buf[0]) * dot(member, held)
+    low_buf[dp] = low.astype(BF16)
+    low_copies = []
+    for d in range(1, peers):
+        copy = pltpu.make_async_remote_copy(
+            src_ref=low_buf.at[dp],
+            dst_ref=low_buf.at[dp],
+            send_sem=low_send.at[d - 1],
+            recv_sem=low_recv.at[d - 1],
+            device_id={"dp": lax.rem(dp + d, peers)},
+            device_id_type=MESH,
+        )
+        copy.start()
+        low_copies.append(copy)
+
+    loads[1].wait()
+    for c in range(chunks):
+        base_buf[:, c * chunk : (c + 1) * chunk] = dot(att, w_buf[:, c * chunk : (c + 1) * chunk])
+    loads[2].wait()
+    for copy in low_copies:
+        copy.wait_recv()
+
+    expanded = jnp.concatenate([low_buf[a] for a in range(peers)], axis=1)
+    part_copies = []
+    for c in range(chunks):
+        at = slice(c * chunk, (c + 1) * chunk)
+        up = up_buf[:, :, at].reshape(peers * low_rank, chunk)
+        total = base_buf[:, at] + dot(expanded, up)
+        part_buf[c] = total.astype(BF16).reshape(blocks, height // blocks, chunk)
+        for d in range(1, blocks):
+            target = lax.rem(tp + d, blocks)
+            copy = pltpu.make_async_remote_copy(
+                src_ref=part_buf.at[c, target],
+                dst_ref=part_recv.at[c, d - 1],
+                send_sem=part_send_sem.at[c, d - 1],
+                recv_sem=part_recv_sem.at[c, d - 1],
+                device_id={"tensor": target},
+                device_id_type=MESH,
+            )
+            copy.start()
+            part_copies.append(copy)
+    for c in range(chunks):
+        total = part_buf[c, tp].astype(F32)
+        for d in range(1, blocks):
+            part_copies[c * (blocks - 1) + d - 1].wait_recv()
+            total = total + part_recv[c, d - 1].astype(F32)
+        mixed_ref[:, c * chunk : (c + 1) * chunk] = total.astype(BF16)
+
+    own.wait()
+    for copy in cache_copies:
+        copy.wait_recv()
+    for copy in att_copies + cache_copies + low_copies + part_copies:
+        copy.wait_send()
+
+
+def fused_shards(
+    peers,
+    blocks,
+    queries,
+    key_value_cache,
+    key_value_lengths,
+    adapter_index,
+    adapter_down_weight,
+    adapter_up_weight,
+    output_weight,
+):
+    count, feats = queries.shape
+    capacity = max(2, 2 * count // peers)
+    row = math.prod(key_value_cache.shape[1:])
+    out_width = output_weight.shape[1]
+    low_rank = adapter_down_weight.shape[1]
+    height = peers * count
+    chunks = 4
+    chunk = out_width // chunks
+    vmem = pl.BlockSpec(memory_space=pltpu.VMEM)
+    hbm = pl.BlockSpec(memory_space=pl.ANY)
+    dma = pltpu.SemaphoreType.DMA
+    mixed, moved = pl.pallas_call(
+        functools.partial(fused_kernel, peers, blocks, key_value_cache.shape[-1]),
+        out_shape=(
+            jax.ShapeDtypeStruct((height // blocks, out_width), BF16),
+            jax.ShapeDtypeStruct((peers, capacity, row), BF16),
+        ),
+        in_specs=[vmem, vmem, vmem, vmem, hbm, hbm, hbm],
+        out_specs=(vmem, hbm),
+        scratch_shapes=[
+            pltpu.VMEM(output_weight.shape, BF16),
+            pltpu.VMEM(adapter_up_weight.shape, BF16),
+            pltpu.VMEM(adapter_down_weight.shape, BF16),
+            pltpu.VMEM((peers, count, feats + LANES), BF16),
+            pltpu.VMEM((peers, capacity, row), BF16),
+            pltpu.VMEM((peers, height, low_rank), BF16),
+            pltpu.VMEM((height, out_width), F32),
+            pltpu.VMEM((chunks, blocks, height // blocks, chunk), BF16),
+            pltpu.VMEM((chunks, blocks - 1, height // blocks, chunk), BF16),
+            dma((4,)),
+            dma((peers - 1,)),
+            dma((peers - 1,)),
+            dma((peers - 1,)),
+            dma((peers - 1,)),
+            dma((peers - 1,)),
+            dma((peers - 1,)),
+            dma((chunks, blocks - 1)),
+            dma((chunks, blocks - 1)),
+        ],
+        compiler_params=pltpu.CompilerParams(
+            collective_id=0, has_side_effects=True, vmem_limit_bytes=56 * 1024 * 1024
+        ),
+        name="fused",
+    )(
+        queries,
+        key_value_cache.reshape(count, row),
+        key_value_lengths.reshape(1, count),
+        adapter_index.reshape(1, count),
+        adapter_down_weight,
+        adapter_up_weight,
+        output_weight,
+    )
+    return mixed, moved.reshape((peers * capacity,) + key_value_cache.shape[1:])
 
 
 def earlier_same(targets):
@@ -95,6 +391,8 @@
 
 
 def solution(mesh):
+    peers, blocks = mesh.shape["dp"], mesh.shape["tensor"]
+    body = functools.partial(fused_shards, peers, blocks) if peers <= 4 else shards
     in_specs = (
         P(("grp", "dp"), "tensor"),
         P(("grp", "dp"), None, None, "tensor"),
@@ -105,4 +403,4 @@
         P("tensor", "dp"),
     )
     out_specs = (P(("grp", "tensor"), "dp"), P(("grp", "dp"), None, None, "tensor"))
-    return jax.shard_map(shards, mesh=mesh, in_specs=in_specs, out_specs=out_specs, check_vma=False)
+    return jax.shard_map(body, mesh=mesh, in_specs=in_specs, out_specs=out_specs, check_vma=False)

time: 112 us -> 46.9 us (0.42)
  blocking collectives: 52.1 us -> 0 us
  Pallas kernels: 0 us -> 40.4 us
  between operations: 14.8 us -> 0.64 us
  waiting for transfers between devices: 13.4 us -> 0 us
  starting transfers between devices: 9.91 us -> 0 us
  matrix products: 6.74 us -> 0 us
  local copies, waits for them, and re-layouts: 10.4 us -> 5.62 us
  other arithmetic: 4.13 us -> 0 us
    pallas_call x0 -> x1, Pallas kernels: none -> 40.4 us  [fused_shards(): pl.pallas_call(functools.partial(fused_kernel, peers, blocks, key_value_c...]
    all_gather x2 -> x0, blocking collectives: 32.9 us -> none  [the longest x1 19.7 us: shards(): part_attended = lax.all_gather(attended_rows, 'dp', axis=0, tiled=True)]
    all_to_all x1 -> x0, blocking collectives: 12.7 us -> none  [shards(): lax.all_to_all(spread(key_value_cache), 'dp', split_axis=0, concat_axis=0...]
    all_to_all x2 -> x0, starting transfers between devices: 9.91 us -> none  [the longest x1 6.45 us: shards(): lax.all_to_all(spread(attended_rows), 'dp', split_axis=0, concat_axis=0,...]
    reduce_scatter x1 -> x0, waiting for transfers between devices: 7.82 us -> none  [shards(): lax.psum_scatter(request_block, 'tensor', scatter_dimension=0, tiled=True)]
    dot_general x5 -> x0, matrix products: 6.74 us -> none  [the longest x1 4.67 us: shards(): jnp.dot(part_attended, output_weight, preferred_element_type=jnp.float32)]
    unnamed x1 -> x0, blocking collectives: 6.59 us -> none
    all_to_all x2 -> x0, waiting for transfers between devices: 5.58 us -> none  [the longest x1 5.58 us: shards(): lax.all_to_all(low_rank_output, 'dp', split_axis=0, concat_axis=0, tiled=...]
  transfers between devices with their start and end apart: 3 -> 0, of which waited for: 2 -> 0; matrix products, arithmetic and copies ran while one was open for 9% -> 0% of each run, Pallas kernels for 0% -> 0%
where the time goes in v1:
time: 46.9 us; the launch traced here: 46.6 us
  Pallas kernels  40.4 us (86%)
  local copies, waits for them, and re-layouts  5.62 us (12%)
  between operations  0.64 us (1%)
    pallas_call x1, Pallas kernels, fused_shards(): pl.pallas_call(functools.partial(fused_kernel, peers, blocks, key_value_c...  40.4 us
    reshape x1, local copies, waits for them, and re-layouts, fused_shards(): moved.reshape((peers * capacity,) + key_value_cache.shape[1:])  2.22 us
    reshape x1, local copies, waits for them, and re-layouts, fused_shards(): key_value_cache.reshape(count, row)  1.83 us
    unnamed x1, local copies, waits for them, and re-layouts  1.57 us

profile of v1, /device:TPU:0, one launch (start us, length us, event | category | flops | bytes accessed | tf_op | source)
XLA Modules:
  0.0 46.6 jit_solution(8368483881574632150)
XLA Ops:
  0.6 1.8 %reshape.16.cache_ref = bf16[32,4096]{1,0:T(8,128)(2,1)} reshape(bf16[32,8,2,256]{3,2,1,0:T(2,128)(2,1)} %param.8) | data formatting | bytes 524288 | tf_op jit(solution)/shard_map/reshape | solution.py:297
  2.5 40.4 %fused.1 = (bf16[32,2048]{1,0:T(8,128)(2,1)}, bf16[4,16,4096]{2,1,0:T(8,128)(2,1)}) custom-call(bf16[32,2048]{1,0:T(8,128)(2,1)} %q_ref.1, bf16[32,4096]{1,0:T(8,128)(2,1)} %reshape.16.cache_ref, s32[1,32]{1,0:T(1,128)} %bitcast.2, s32[1,32]{1,0:T(1,128)} %bitcast.3, bf16[1,64,2048]{2,1,0:T(8,128)(2,1)} %down_hbm.1, bf16[4,64,2048]{2,1,0:T(8,128)(2,1)} %up_hbm.1, ...), custom_call_target="tpu_custom_call" | custom-call | tf_op jit(solution)/shard_map/fused/pallas_call | solution.py:263
  42.9 2.2 %reshape.19 = bf16[64,8,2,256]{3,2,1,0:T(2,128)(2,1)} reshape(bf16[4,16,4096]{2,1,0:T(8,128)(2,1)} %get-tuple-element.5) | data formatting | bytes 1048576 | tf_op jit(solution)/shard_map/reshape | solution.py:304
  45.1 1.6 %copy.10 = bf16[32,2048]{1,0:T(8,128)(2,1)} copy(bf16[32,2048]{1,0:T(8,128)(2,1)} %get-tuple-element.8) | data formatting | bytes 262144

commit v2 on v1

--- a/solution.py
+++ b/solution.py
@@ -10,6 +10,7 @@
 
 HD = 128
 LANES = 128
+CACHE_STEP = 3
 MESH = pl.DeviceIdType.MESH
 F32 = jnp.float32
 BF16 = jnp.bfloat16
@@ -50,7 +51,8 @@
     att_buf,
     spread_buf,
     low_buf,
-    base_buf,
+    low_in,
+    own_buf,
     part_buf,
     part_recv,
     load_sem,
@@ -68,8 +70,8 @@
     count, feats = q_ref.shape
     capacity = spread_buf.shape[1]
     out_width = w_buf.shape[1]
-    chunks = part_recv.shape[0]
-    chunk = out_width // chunks
+    chunk = part_buf.shape[3]
+    chunks = out_width // chunk
     kv_heads = width // HD
     group = feats // width
     positions = cache_ref.shape[1] // (2 * width)
@@ -83,14 +85,15 @@
         load.start()
 
     barrier = pltpu.get_barrier_semaphore()
-    for d in range(1, peers):
-        pl.semaphore_signal(
-            barrier, inc=1, device_id={"dp": lax.rem(dp + d, peers)}, device_id_type=MESH
-        )
-    for d in range(1, blocks):
-        pl.semaphore_signal(
-            barrier, inc=1, device_id={"tensor": lax.rem(tp + d, blocks)}, device_id_type=MESH
-        )
+    for d in range(peers):
+        for e in range(blocks):
+            if d or e:
+                pl.semaphore_signal(
+                    barrier,
+                    inc=1,
+                    device_id={"dp": lax.rem(dp + d, peers), "tensor": lax.rem(tp + e, blocks)},
+                    device_id_type=MESH,
+                )
 
     rows, cols = group * count, positions * count
     row_request = iota((rows, cols), 0) & (count - 1)
@@ -135,19 +138,29 @@
     eye = flag(iota((count, count), 0) == iota((count, count), 1))
     att_buf[dp, :, feats : feats + LANES] = nt_dot(eye, chosen_flag).astype(BF16)
 
-    pl.semaphore_wait(barrier, peers - 1 + blocks - 1)
-    att_copies = []
-    for d in range(1, peers):
-        copy = pltpu.make_async_remote_copy(
-            src_ref=att_buf.at[dp],
-            dst_ref=att_buf.at[dp],
-            send_sem=att_send.at[d - 1],
-            recv_sem=att_recv.at[d - 1],
-            device_id={"dp": lax.rem(dp + d, peers)},
+    pl.semaphore_wait(barrier, peers * blocks - 1)
+
+    def att_copy(source, way):
+        return pltpu.make_async_remote_copy(
+            src_ref=att_buf.at[source],
+            dst_ref=att_buf.at[source],
+            send_sem=att_send.at[source, way],
+            recv_sem=att_recv.at[source],
+            device_id={"dp": lax.rem(dp + (1 if way else peers - 1), peers)},
             device_id_type=MESH,
         )
-        copy.start()
-        att_copies.append(copy)
+
+    def pass_on(source, act):
+        @pl.when((source <= dp) & (dp < peers - 1))
+        def _():
+            act(att_copy(source, 1))
+
+        @pl.when((source >= dp) & (dp > 0))
+        def _():
+            act(att_copy(source, 0))
+
+    others = [lax.rem(dp + d, peers) for d in range(1, peers)]
+    pass_on(dp, lambda copy: copy.start())
 
     earlier = flag(iota((count, count), 0) < iota((count, count), 1))
     before = dot(chosen_flag, earlier)
@@ -159,83 +172,146 @@
     for c in range(cache_ref.shape[1] // step):
         piece = dot(move, cache_ref[:, c * step : (c + 1) * step]).astype(BF16)
         spread_buf[:, :, c * step : (c + 1) * step] = piece.reshape(peers, capacity, step)
-    cache_copies = []
-    for d in range(1, peers):
-        target = lax.rem(dp + d, peers)
-        copy = pltpu.make_async_remote_copy(
+
+    def cache_copy(target, source):
+        return pltpu.make_async_remote_copy(
             src_ref=spread_buf.at[target],
-            dst_ref=moved_ref.at[dp],
-            send_sem=cache_send.at[d - 1],
-            recv_sem=cache_recv.at[d - 1],
+            dst_ref=moved_ref.at[source],
+            send_sem=cache_send.at[target],
+            recv_sem=cache_recv.at[source],
             device_id={"dp": target},
             device_id_type=MESH,
         )
-        copy.start()
-        cache_copies.append(copy)
+
     own = pltpu.make_async_copy(spread_buf.at[dp], moved_ref.at[dp], load_sem.at[3])
     own.start()
 
-    for copy in att_copies:
-        copy.wait_recv()
-    height = peers * count
-    att = att_buf[:, :, :feats].reshape(height, feats)
-    member = att_buf[:, :, feats : feats + LANES].reshape(height, LANES)
-    loads[0].wait()
+    def low_copy(block, target, holder, part):
+        return pltpu.make_async_remote_copy(
+            src_ref=low_buf.at[block],
+            dst_ref=low_in.at[holder, part],
+            send_sem=low_send.at[block, target],
+            recv_sem=low_recv.at[holder, part],
+            device_id={"dp": target, "tensor": block},
+            device_id_type=MESH,
+        )
+
+    def part_copy(block, part, c):
+        return pltpu.make_async_remote_copy(
+            src_ref=part_buf.at[block, c],
+            dst_ref=part_recv.at[part, c],
+            send_sem=part_send_sem.at[block, c],
+            recv_sem=part_recv_sem.at[part, c],
+            device_id={"tensor": block},
+            device_id_type=MESH,
+        )
+
     low_rank = down_buf.shape[1]
     held = flag(iota((LANES, low_rank), 0) == dp)
-    low = nt_dot(att, down_buf[0]) * dot(member, held)
-    low_buf[dp] = low.astype(BF16)
-    low_copies = []
-    for d in range(1, peers):
-        copy = pltpu.make_async_remote_copy(
-            src_ref=low_buf.at[dp],
-            dst_ref=low_buf.at[dp],
-            send_sem=low_send.at[d - 1],
-            recv_sem=low_recv.at[d - 1],
-            device_id={"dp": lax.rem(dp + d, peers)},
-            device_id_type=MESH,
-        )
-        copy.start()
-        low_copies.append(copy)
-
+    loads[0].wait()
     loads[1].wait()
-    for c in range(chunks):
-        base_buf[:, c * chunk : (c + 1) * chunk] = dot(att, w_buf[:, c * chunk : (c + 1) * chunk])
+
+    def nearest(step):
+        up = jnp.where(step - 1 < dp, step - 1, step)
+        last = peers - step
+        down = jnp.where(last > dp, last, last - 1)
+        return jnp.where(step == 0, dp, jnp.where(dp < peers // 2, up, down))
+
+    def arrive(step):
+        source = nearest(step)
+        att_copy(source, 0).wait_recv()
+        pass_on(source, lambda copy: copy.start())
+
+    inner = (dp > 0) & (dp < peers - 1)
+
+    def work(step, carry):
+        source = nearest(step)
+
+        @pl.when((step > 0) & jnp.logical_not(inner & (step == 2)))
+        def _():
+            arrive(step)
+
+        @pl.when((step == 1) & inner)
+        def _():
+            arrive(2)
+
+        rows = att_buf[source, :, :feats]
+        member = dot(att_buf[source, :, feats : feats + LANES], held)
+        low_buf[source] = (nt_dot(rows, down_buf[0]) * member).astype(BF16)
+        for target in others:
+            low_copy(source, target, dp, tp).start()
+
+        @pl.when(source != tp)
+        def _():
+            low_copy(source, dp, dp, tp).start()
+
+        @pl.when(source == tp)
+        def _():
+            low_in[dp, tp] = low_buf[source]
+
+        @pl.when(step == CACHE_STEP)
+        def _():
+            for target in others:
+                cache_copy(target, dp).start()
+
+        for c in range(chunks):
+            at = slice(c * chunk, (c + 1) * chunk)
+            part = dot(rows, w_buf[:, at])
+            part_buf[source, c] = part.astype(BF16)
+
+            @pl.when(source == tp)
+            def _():
+                own_buf[:, at] = part
+
+            @pl.when(source != tp)
+            def _():
+                part_copy(source, tp, c).start()
+
+        return carry
+
+    lax.fori_loop(0, peers, work, 0)
+
     loads[2].wait()
-    for copy in low_copies:
-        copy.wait_recv()
-
-    expanded = jnp.concatenate([low_buf[a] for a in range(peers)], axis=1)
-    part_copies = []
+    for d in range(peers):
+        for e in range(blocks):
+            if d or e:
+                low_copy(tp, dp, lax.rem(dp + d, peers), lax.rem(tp + e, blocks)).wait_recv()
+    lows = []
+    for a in range(peers):
+        total = low_in[a, 0].astype(F32)
+        for t in range(1, blocks):
+            total = total + low_in[a, t].astype(F32)
+        lows.append(total)
+    low_total = jnp.concatenate(lows, axis=1)
+    high = low_total.astype(BF16)
+    rest = (low_total - high.astype(F32)).astype(BF16)
+    both = jnp.concatenate([high, rest], axis=0)
     for c in range(chunks):
         at = slice(c * chunk, (c + 1) * chunk)
-        up = up_buf[:, :, at].reshape(peers * low_rank, chunk)
-        total = base_buf[:, at] + dot(expanded, up)
-        part_buf[c] = total.astype(BF16).reshape(blocks, height // blocks, chunk)
-        for d in range(1, blocks):
-            target = lax.rem(tp + d, blocks)
-            copy = pltpu.make_async_remote_copy(
-                src_ref=part_buf.at[c, target],
-                dst_ref=part_recv.at[c, d - 1],
-                send_sem=part_send_sem.at[c, d - 1],
-                recv_sem=part_recv_sem.at[c, d - 1],
-                device_id={"tensor": target},
-                device_id_type=MESH,
-            )
-            copy.start()
-            part_copies.append(copy)
+        delta = dot(both, up_buf[:, :, at].reshape(peers * low_rank, chunk))
+        own_buf[:, at] += delta[:count] + delta[count:]
+    parts = [lax.rem(tp + e, blocks) for e in range(1, blocks)]
     for c in range(chunks):
-        total = part_buf[c, tp].astype(F32)
-        for d in range(1, blocks):
-            part_copies[c * (blocks - 1) + d - 1].wait_recv()
-            total = total + part_recv[c, d - 1].astype(F32)
-        mixed_ref[:, c * chunk : (c + 1) * chunk] = total.astype(BF16)
+        at = slice(c * chunk, (c + 1) * chunk)
+        total = own_buf[:, at]
+        for part in parts:
+            part_copy(tp, part, c).wait_recv()
+            total = total + part_recv[part, c].astype(F32)
+        mixed_ref[:, at] = total.astype(BF16)
 
     own.wait()
-    for copy in cache_copies:
-        copy.wait_recv()
-    for copy in att_copies + cache_copies + low_copies + part_copies:
-        copy.wait_send()
+    for source in others:
+        cache_copy(dp, source).wait_recv()
+    for target in others:
+        cache_copy(target, dp).wait_send()
+    for block in parts:
+        for c in range(chunks):
+            part_copy(block, tp, c).wait_send()
+        low_copy(block, dp, dp, tp).wait_send()
+    for block in range(blocks):
+        pass_on(block, lambda copy: copy.wait_send())
+        for target in others:
+            low_copy(block, target, dp, tp).wait_send()
 
 
 def fused_shards(
@@ -255,8 +331,7 @@
     out_width = output_weight.shape[1]
     low_rank = adapter_down_weight.shape[1]
     height = peers * count
-    chunks = 4
-    chunk = out_width // chunks
+    chunks = 2
     vmem = pl.BlockSpec(memory_space=pltpu.VMEM)
     hbm = pl.BlockSpec(memory_space=pl.ANY)
     dma = pltpu.SemaphoreType.DMA
@@ -274,19 +349,20 @@
             pltpu.VMEM(adapter_down_weight.shape, BF16),
             pltpu.VMEM((peers, count, feats + LANES), BF16),
             pltpu.VMEM((peers, capacity, row), BF16),
-            pltpu.VMEM((peers, height, low_rank), BF16),
-            pltpu.VMEM((height, out_width), F32),
-            pltpu.VMEM((chunks, blocks, height // blocks, chunk), BF16),
-            pltpu.VMEM((chunks, blocks - 1, height // blocks, chunk), BF16),
+            pltpu.VMEM((blocks, count, low_rank), BF16),
+            pltpu.VMEM((peers, blocks, count, low_rank), BF16),
+            pltpu.VMEM((count, out_width), F32),
+            pltpu.VMEM((blocks, chunks, count, out_width // chunks), BF16),
+            pltpu.VMEM((blocks, chunks, count, out_width // chunks), BF16),
             dma((4,)),
-            dma((peers - 1,)),
-            dma((peers - 1,)),
-            dma((peers - 1,)),
-            dma((peers - 1,)),
-            dma((peers - 1,)),
-            dma((peers - 1,)),
-            dma((chunks, blocks - 1)),
-            dma((chunks, blocks - 1)),
+            dma((peers, 2)),
+            dma((peers,)),
+            dma((peers,)),
+            dma((peers,)),
+            dma((blocks, peers)),
+            dma((peers, blocks)),
+            dma((blocks, chunks)),
+            dma((blocks, chunks)),
         ],
         compiler_params=pltpu.CompilerParams(
             collective_id=0, has_side_effects=True, vmem_limit_bytes=56 * 1024 * 1024
@@ -392,7 +468,7 @@
 
 def solution(mesh):
     peers, blocks = mesh.shape["dp"], mesh.shape["tensor"]
-    body = functools.partial(fused_shards, peers, blocks) if peers <= 4 else shards
+    body = functools.partial(fused_shards, peers, blocks) if peers == blocks <= 4 else shards
     in_specs = (
         P(("grp", "dp"), "tensor"),
         P(("grp", "dp"), None, None, "tensor"),

time: 46.9 us -> 39.2 us (0.84)
  Pallas kernels: 40.4 us -> 32.7 us
    pallas_call x1, Pallas kernels: 40.4 us -> 32.7 us  [fused_shards(): pl.pallas_call(functools.partial(fused_kernel, peers, blocks, key_value_c...]
where the time goes in v2:
time: 39.2 us; the launch traced here: 39 us
  Pallas kernels  32.7 us (83%)
  local copies, waits for them, and re-layouts  5.62 us (14%)
  between operations  0.64 us (2%)
    pallas_call x1, Pallas kernels, fused_shards(): pl.pallas_call(functools.partial(fused_kernel, peers, blocks, key_value_c...  32.7 us
    reshape x1, local copies, waits for them, and re-layouts, fused_shards(): moved.reshape((peers * capacity,) + key_value_cache.shape[1:])  2.22 us
    reshape x1, local copies, waits for them, and re-layouts, fused_shards(): key_value_cache.reshape(count, row)  1.83 us
    unnamed x1, local copies, waits for them, and re-layouts  1.57 us

profile of v2, /device:TPU:0, one launch (start us, length us, event | category | flops | bytes accessed | tf_op | source)
XLA Modules:
  0.0 39.0 jit_solution(2354394099813294141)
XLA Ops:
  0.6 1.8 %reshape.16.cache_ref = bf16[32,4096]{1,0:T(8,128)(2,1)} reshape(bf16[32,8,2,256]{3,2,1,0:T(2,128)(2,1)} %param.8) | data formatting | bytes 524288 | tf_op jit(solution)/shard_map/reshape | solution.py:373
  2.5 32.7 %fused.1 = (bf16[32,2048]{1,0:T(8,128)(2,1)}, bf16[4,16,4096]{2,1,0:T(8,128)(2,1)}) custom-call(bf16[32,2048]{1,0:T(8,128)(2,1)} %q_ref.1, bf16[32,4096]{1,0:T(8,128)(2,1)} %reshape.16.cache_ref, s32[1,32]{1,0:T(1,128)} %bitcast.2, s32[1,32]{1,0:T(1,128)} %bitcast.3, bf16[1,64,2048]{2,1,0:T(8,128)(2,1)} %down_hbm.1, bf16[4,64,2048]{2,1,0:T(8,128)(2,1)} %up_hbm.1, ...), custom_call_target="tpu_custom_call" | custom-call | tf_op jit(solution)/shard_map/fused/pallas_call | solution.py:338
  35.2 2.2 %reshape.19 = bf16[64,8,2,256]{3,2,1,0:T(2,128)(2,1)} reshape(bf16[4,16,4096]{2,1,0:T(8,128)(2,1)} %get-tuple-element.5) | data formatting | bytes 1048576 | tf_op jit(solution)/shard_map/reshape | solution.py:380
  37.4 1.6 %copy.10 = bf16[32,2048]{1,0:T(8,128)(2,1)} copy(bf16[32,2048]{1,0:T(8,128)(2,1)} %get-tuple-element.8) | data formatting | bytes 262144

commit v3 on v2

--- a/solution.py
+++ b/solution.py
@@ -222,6 +222,7 @@
         att_copy(source, 0).wait_recv()
         pass_on(source, lambda copy: copy.start())
 
+    inward = jnp.where(dp < peers // 2, lax.rem(dp + 1, peers), jnp.maximum(dp - 1, 0))
     inner = (dp > 0) & (dp < peers - 1)
 
     def work(step, carry):
@@ -234,6 +235,18 @@
         @pl.when((step == 1) & inner)
         def _():
             arrive(2)
+
+        @pl.when(step == CACHE_STEP - 1)
+        def _():
+            cache_copy(inward, dp).start()
+
+        @pl.when(step == CACHE_STEP)
+        def _():
+            for target in others:
+
+                @pl.when(target != inward)
+                def _():
+                    cache_copy(target, dp).start()
 
         rows = att_buf[source, :, :feats]
         member = dot(att_buf[source, :, feats : feats + LANES], held)
@@ -248,11 +261,6 @@
         @pl.when(source == tp)
         def _():
             low_in[dp, tp] = low_buf[source]
-
-        @pl.when(step == CACHE_STEP)
-        def _():
-            for target in others:
-                cache_copy(target, dp).start()
 
         for c in range(chunks):
             at = slice(c * chunk, (c + 1) * chunk)
@@ -468,7 +476,7 @@
 
 def solution(mesh):
     peers, blocks = mesh.shape["dp"], mesh.shape["tensor"]
-    body = functools.partial(fused_shards, peers, blocks) if peers == blocks <= 4 else shards
+    body = functools.partial(fused_shards, peers, blocks) if peers == blocks == CACHE_STEP + 1 else shards
     in_specs = (
         P(("grp", "dp"), "tensor"),
         P(("grp", "dp"), None, None, "tensor"),

time: 39.2 us -> 38.6 us (0.985)
  Pallas kernels: 32.7 us -> 32.1 us
    pallas_call x1, Pallas kernels: 32.7 us -> 32.1 us  [fused_shards(): pl.pallas_call(functools.partial(fused_kernel, peers, blocks, key_value_c...]
where the time goes in v3:
time: 38.6 us; the launch traced here: 38.4 us
  Pallas kernels  32.1 us (83%)
  local copies, waits for them, and re-layouts  5.62 us (15%)
  between operations  0.64 us (2%)
    pallas_call x1, Pallas kernels, fused_shards(): pl.pallas_call(functools.partial(fused_kernel, peers, blocks, key_value_c...  32.1 us
    reshape x1, local copies, waits for them, and re-layouts, fused_shards(): moved.reshape((peers * capacity,) + key_value_cache.shape[1:])  2.22 us
    reshape x1, local copies, waits for them, and re-layouts, fused_shards(): key_value_cache.reshape(count, row)  1.83 us
    unnamed x1, local copies, waits for them, and re-layouts  1.57 us

profile of v3, /device:TPU:0, one launch (start us, length us, event | category | flops | bytes accessed | tf_op | source)
XLA Modules:
  0.0 38.4 jit_solution(16690557478086931741)
XLA Ops:
  0.6 1.8 %reshape.16.cache_ref = bf16[32,4096]{1,0:T(8,128)(2,1)} reshape(bf16[32,8,2,256]{3,2,1,0:T(2,128)(2,1)} %param.8) | data formatting | bytes 524288 | tf_op jit(solution)/shard_map/reshape | solution.py:381
  2.5 32.1 %fused.1 = (bf16[32,2048]{1,0:T(8,128)(2,1)}, bf16[4,16,4096]{2,1,0:T(8,128)(2,1)}) custom-call(bf16[32,2048]{1,0:T(8,128)(2,1)} %q_ref.1, bf16[32,4096]{1,0:T(8,128)(2,1)} %reshape.16.cache_ref, s32[1,32]{1,0:T(1,128)} %bitcast.2, s32[1,32]{1,0:T(1,128)} %bitcast.3, bf16[1,64,2048]{2,1,0:T(8,128)(2,1)} %down_hbm.1, bf16[4,64,2048]{2,1,0:T(8,128)(2,1)} %up_hbm.1, ...), custom_call_target="tpu_custom_call" | custom-call | tf_op jit(solution)/shard_map/fused/pallas_call | solution.py:346
  34.6 2.2 %reshape.19 = bf16[64,8,2,256]{3,2,1,0:T(2,128)(2,1)} reshape(bf16[4,16,4096]{2,1,0:T(8,128)(2,1)} %get-tuple-element.5) | data formatting | bytes 1048576 | tf_op jit(solution)/shard_map/reshape | solution.py:388
  36.8 1.6 %copy.10 = bf16[32,2048]{1,0:T(8,128)(2,1)} copy(bf16[32,2048]{1,0:T(8,128)(2,1)} %get-tuple-element.8) | data formatting | bytes 262144

commit v4 on v3

--- a/solution.py
+++ b/solution.py
@@ -159,7 +159,7 @@
         def _():
             act(att_copy(source, 0))
 
-    others = [lax.rem(dp + d, peers) for d in range(1, peers)]
+    others = [lax.rem(dp + d, peers) for d in sorted(range(1, peers), key=lambda d: -min(d, peers - d))]
     pass_on(dp, lambda copy: copy.start())
 
     earlier = flag(iota((count, count), 0) < iota((count, count), 1))

time: 38.6 us -> 38.5 us (level)
  no operation moved by 1% of the time
where the time goes in v4:
time: 38.5 us; the launch traced here: 38.3 us
  Pallas kernels  32 us (83%)
  local copies, waits for them, and re-layouts  5.62 us (15%)
  between operations  0.64 us (2%)
    pallas_call x1, Pallas kernels, fused_shards(): pl.pallas_call(functools.partial(fused_kernel, peers, blocks, key_value_c...  32 us
    reshape x1, local copies, waits for them, and re-layouts, fused_shards(): moved.reshape((peers * capacity,) + key_value_cache.shape[1:])  2.22 us
    reshape x1, local copies, waits for them, and re-layouts, fused_shards(): key_value_cache.reshape(count, row)  1.83 us
    unnamed x1, local copies, waits for them, and re-layouts  1.57 us

profile of v4, /device:TPU:0, one launch (start us, length us, event | category | flops | bytes accessed | tf_op | source)
XLA Modules:
  0.0 38.3 jit_solution(5494201021626326470)
XLA Ops:
  0.6 1.8 %reshape.16.cache_ref = bf16[32,4096]{1,0:T(8,128)(2,1)} reshape(bf16[32,8,2,256]{3,2,1,0:T(2,128)(2,1)} %param.8) | data formatting | bytes 524288 | tf_op jit(solution)/shard_map/reshape | solution.py:381
  2.5 32.0 %fused.1 = (bf16[32,2048]{1,0:T(8,128)(2,1)}, bf16[4,16,4096]{2,1,0:T(8,128)(2,1)}) custom-call(bf16[32,2048]{1,0:T(8,128)(2,1)} %q_ref.1, bf16[32,4096]{1,0:T(8,128)(2,1)} %reshape.16.cache_ref, s32[1,32]{1,0:T(1,128)} %bitcast.2, s32[1,32]{1,0:T(1,128)} %bitcast.3, bf16[1,64,2048]{2,1,0:T(8,128)(2,1)} %down_hbm.1, bf16[4,64,2048]{2,1,0:T(8,128)(2,1)} %up_hbm.1, ...), custom_call_target="tpu_custom_call" | custom-call | tf_op jit(solution)/shard_map/fused/pallas_call | solution.py:346
  34.5 2.2 %reshape.19 = bf16[64,8,2,256]{3,2,1,0:T(2,128)(2,1)} reshape(bf16[4,16,4096]{2,1,0:T(8,128)(2,1)} %get-tuple-element.5) | data formatting | bytes 1048576 | tf_op jit(solution)/shard_map/reshape | solution.py:388
  36.7 1.6 %copy.10 = bf16[32,2048]{1,0:T(8,128)(2,1)} copy(bf16[32,2048]{1,0:T(8,128)(2,1)} %get-tuple-element.8) | data formatting | bytes 262144
